TPU v7x, 32 devices: a whole 2x2x4 slice. The times are simulated.
32 devices in a mesh: scen: 2 (over y), blk: 16 (over z, x, core).
Axes of the slice: x: 2, y: 2, z: 4, core: 2. Of those that a mesh axis runs over, the one named last changes fastest.
Arguments:
- returns: bfloat16 [128, 8192], P(('scen', 'blk')), may hold values from -6 to 6
- vol_hist: float32 [128, 8192], P(('scen', 'blk')), may hold values from 0.5 to 5.5, as said below
- vol_now: float32 [8192], replicated, may hold values from 0.5 to 2
- sensitivity: bfloat16 [4096, 128, 128], P('blk'), may hold values from -0.109375 to 0.109375
- block_pairs: int32 [4096, 3], P('blk'), may hold values from 0 to 63, as said below
- book_order: int32 [32], replicated, may hold values from 0 to 31, each once
Outputs:
- profit_loss: float32 [128, 4096], P('scen', 'blk')
- book_rms: float32 [4096], P('blk')
Inputs may be any that keep to these rules, and one draw needn't show every extreme that they name: `block_pairs`: each index k of blk holds 256 slots; their factor blocks lie in k * 4 to k * 4 + 3; on each index the live slots come first; some index has all 256 slots live. `vol_hist`: positive volatilities.
All inputs are finite; a program needn't handle non-finite values.
Results may differ from a plain program's by a relative error of at most 0.0029.
Values may be sent and summed in bfloat16 or wider, within the bound.
No kernel may reach another device: no remote copies, remote signals or barrier semaphores. Data moves between devices by JAX's collectives and lax.ppermute only.
A program may use at most 64 MiB of HBM per device.

v0:
```python
import functools

import jax
import jax.numpy as jnp
from jax import lax
from jax.experimental import pallas as pl
from jax.experimental.pallas import tpu as pltpu
from jax.sharding import PartitionSpec as P

UNROLL = 32
SIZES = (4, 2, 2, 4, 2, 2)
LAG = 6
AHEAD = 2
PIECES = 4
VMEM_LIMIT = 32 * 1024 * 1024
VMEM = pl.BlockSpec(memory_space=pltpu.VMEM)
HBM = pl.BlockSpec(memory_space=pltpu.HBM)


def accumulate(
    groups, shocks, pairs_hbm, order_hbm, sens_hbm, kept, sent, acc, sens, pairs, order, position, small, arrived
):
    slots = sens.shape[0]
    factors = shocks.shape[0]
    chunks = arrived.shape[0]
    chunk = slots // chunks
    half = kept.shape[0]
    books = 2 * half
    per_owner = books // groups
    index = lax.axis_index("blk")
    core = index & 1

    def fetch(c):
        span = pl.ds(c * chunk, chunk)
        return pltpu.make_async_copy(sens_hbm.at[span], sens.at[span], arrived.at[c])

    def begin(c, carry):
        part = chunk // PIECES
        for j in range(PIECES):
            span = pl.ds(c * chunk + j * part, part)
            pltpu.make_async_copy(sens_hbm.at[span], sens.at[span], arrived.at[c]).start()
        return carry

    get_order = pltpu.make_async_copy(order_hbm, order, small.at[0])
    get_pairs = pltpu.make_async_copy(pairs_hbm, pairs.at[:, pl.ds(0, slots)], small.at[1])
    get_order.start()
    get_pairs.start()
    for c in range(AHEAD):
        begin(c, 0)
    acc[...] = jnp.zeros_like(acc)
    position[books] = books
    first_factor = index * factors
    for u in range(chunk):
        pairs[0, slots + u] = first_factor
        pairs[1, slots + u] = 0
        pairs[2, slots + u] = 0
    padding = chunks
    rows, block = shocks.shape[1:]
    none = jnp.zeros((rows, block), shocks.dtype)
    blank = jnp.zeros((block, block), sens.dtype)

    packs = []
    for j, size in enumerate(SIZES):
        for unit in range(2):
            first = unit * (chunk // 2) + sum(SIZES[:j])
            packs.append((first, size, unit, j % 2))
    many = len(packs)

    def on_units(*units):
        def push(i, rhs):
            _, _, unit, staged = packs[i]
            pltpu.matmul_push_rhs(rhs, staged, unit)

        def stage(c, i):
            k = c * chunk + packs[i][0]
            if packs[i][1] == 4:
                tiles = [[sens[k], sens[k + 1]], [sens[k + 2], sens[k + 3]]]
            else:
                tiles = [[sens[k], blank], [blank, sens[k + 1]]]
            push(i, jnp.concatenate([jnp.concatenate(row, axis=1) for row in tiles], axis=0))

        def multiply(c, i):
            first, size, _, staged = packs[i]
            scenarios = [shocks[pairs[0, c * chunk + first + t] - first_factor] for t in range(size)]
            if size == 4:
                passes = [[x, none] if t < 2 else [none, x] for t, x in enumerate(scenarios)]
            else:
                passes = [scenarios]
            for t, halves in enumerate(passes):
                target = units[spot[i] + t]
                pltpu.matmul_acc_lhs(target, jnp.concatenate(halves, axis=1), load_staged_rhs=None if t else staged)

        def collect(c, i):
            first, size, _, _ = packs[i]
            popped = [pltpu.matmul_pop(units[spot[i] + t]) for t in range(4 if size == 4 else 1)]
            for t in range(size):
                k = c * chunk + first + t
                book = jnp.where(pairs[2, k] != 0, pairs[1, k], books)
                side = (t % 2) * block
                acc[position[book]] += popped[t if size == 4 else 0][:, side : side + block]

        zeros = jnp.zeros((2 * block, 2 * block), sens.dtype)
        for i in range(many - LAG, many):
            push(i, zeros)
            if i < many - 2:
                multiply(padding, i)

        def work(c, carry):
            fetch(c).wait()
            before = jnp.where(c == 0, padding, c - 1)
            for i in range(many):
                stage(c, i)
                multiply(*((before, i - 2 + many) if i < 2 else (c, i - 2)))
                collect(*((before, i - LAG + many) if i < LAG else (c, i - LAG)))
            return carry

        get_pairs.wait()

        def count(c, busy):
            return busy + jnp.where(pairs[2, c * chunk] != 0, 1, 0)

        busy = lax.fori_loop(0, chunks, count, 0)

        lax.fori_loop(AHEAD, busy, begin, 0)
        get_order.wait()
        for p in range(books):
            owner = p // per_owner
            place = (owner // 2) * per_owner + p % per_owner
            position[order[p]] = place + half * ((owner & 1) ^ core)
        lax.fori_loop(0, busy, work, 0)
        last = jnp.where(busy == 0, padding, busy - 1)
        for i in range(many - 2, many):
            multiply(last, i)
        for i in range(many - LAG, many):
            collect(last, i)

        def drop(c, carry):
            fetch(c).wait()
            return carry

        lax.fori_loop(busy, AHEAD, drop, 0)

    spot = []
    held = []
    for _, size, unit, _ in packs:
        spot.append(len(held))
        held += [pltpu.ACC(unit)((rows, 2 * block), jnp.float32)] * (4 if size == 4 else 1)
    pl.run_scoped(on_units, *held)
    kept[...] = acc[:half]
    sent[...] = acc[half:books].astype(sent.dtype)


def shards(returns, vol_hist, vol_now, sensitivity, block_pairs, book_order):
    groups = lax.axis_size("blk")
    own_rows, width = returns.shape
    slots, block, _ = sensitivity.shape
    own = width // groups
    rows = groups * own_rows
    books = book_order.shape[0]
    siblings = [(i, i ^ 1) for i in range(groups)]
    rescaled = (returns.astype(jnp.float32) * vol_now[None, :] / vol_hist).astype(jnp.bfloat16)
    outgoing = rescaled.reshape(own_rows, groups, own).swapaxes(0, 1)
    incoming = lax.all_to_all(outgoing, "blk", 0, 0)
    shocks = incoming.reshape(rows, own // block, block).transpose(1, 0, 2)
    chunks = slots // UNROLL
    kept, sent = pl.pallas_call(
        functools.partial(accumulate, groups),
        in_specs=[VMEM, HBM, HBM, HBM],
        out_specs=[VMEM, VMEM],
        out_shape=[
            jax.ShapeDtypeStruct((books // 2, rows, block), jnp.float32),
            jax.ShapeDtypeStruct((books // 2, rows, block), jnp.bfloat16),
        ],
        scratch_shapes=[
            pltpu.VMEM((books + 1, rows, block), jnp.float32),
            pltpu.VMEM(sensitivity.shape, sensitivity.dtype),
            pltpu.SMEM((3, slots + UNROLL), jnp.int32),
            pltpu.SMEM((books,), jnp.int32),
            pltpu.SMEM((books + 1,), jnp.int32),
            pltpu.SemaphoreType.DMA((2,)),
            pltpu.SemaphoreType.DMA((chunks,)),
        ],
        compiler_params=pltpu.CompilerParams(vmem_limit_bytes=VMEM_LIMIT),
        cost_estimate=pl.CostEstimate(
            flops=2 * slots * rows * block * block,
            bytes_accessed=2 * slots * block * block,
            transcendentals=0,
        ),
    )(shocks, *(pltpu.with_memory_space_constraint(x, pltpu.HBM) for x in (block_pairs.T, book_order, sensitivity)))
    across = lax.ppermute(sent, "blk", siblings)
    per_owner = books // groups
    chips = groups // 2
    chip_sum = (kept + across.astype(jnp.float32)).astype(jnp.bfloat16).reshape(chips, per_owner, rows, block)
    same_core = [list(range(c, groups, 2)) for c in range(2)]
    arrived = lax.all_to_all(chip_sum, "blk", 0, 0, axis_index_groups=same_core)
    owned = jnp.sum(arrived.astype(jnp.float32), axis=0)
    profit_loss = owned.transpose(1, 0, 2).reshape(rows, per_owner * block)
    spans = lax.axis_size("scen")
    squares = jnp.sum(owned * owned, axis=1).reshape(-1)
    if spans == 2:
        squares = squares + lax.ppermute(squares, "scen", [(0, 1), (1, 0)])
    else:
        squares = lax.psum(squares, "scen")
    book_rms = jnp.sqrt(squares / (rows * spans) + 1e-06)
    return (profit_loss, book_rms)


def solution(mesh):
    def on_mesh(*args):
        with jax.sharding.use_abstract_mesh(mesh.abstract_mesh):
            return whole(*args)

    whole = jax.shard_map(
        shards,
        mesh=mesh,
        in_specs=(
            P(("scen", "blk"), None),
            P(("scen", "blk"), None),
            P(),
            P("blk", None, None),
            P("blk", None),
            P(),
        ),
        out_specs=(P("scen", "blk"), P("blk")),
        check_vma=False,
    )
    return on_mesh
```

profile of v0, /device:TPU:0, one launch (start us, length us, event | category | flops | bytes accessed | tf_op | source)
XLA Modules:
  0.0 36.6 jit_solution(4953015229287059370)
XLA Ops:
  0.6 1.0 %fusion = bf16[4,8192]{1,0:T(4,128)(2,1)S(1)} fusion(f32[4,8192]{1,0:T(4,128)} %param.7, bf16[4,8192]{1,0:T(4,128)(2,1)} %param.6, f32[8192]{0:T(1024)} %param.8), kind=kLoop, calls=%fused_computation.3 | loop fusion | flops 131072 | bytes 294912 | tf_op jit(solution)/shard_map/convert_element_type | solution.py:161
  1.6 14.1 %all_to_all.10 = bf16[16,4,512]{2,1,0:T(4,128)(2,1)S(1)} all-to-all(bf16[16,4,512]{2,1,0:T(4,128)(2,1)S(1)} %bitcast.18), channel_id=1, replica_groups=mesh['scen'=2,'blk'=16] {'blk'}, dimensions={0} | all-to-all | bytes 131072 | tf_op jit(solution)/shard_map/all_to_all | solution.py:163
  15.7 2.8 %shard_map.77 = (f32[16,64,128]{2,1,0:T(8,128)S(1)}, bf16[16,64,128]{2,1,0:T(8,128)(2,1)S(1)}) custom-call(bf16[4,64,128]{2,1,0:T(8,128)(2,1)S(1)} %bitcast.16, s32[3,256]{1,0:T(4,128)} %bitcast.19, s32[32]{0:T(128)} %order_hbm.1, bf16[256,128,128]{2,1,0:T(8,128)(2,1)} %sens_hbm.1), custom_call_target="tpu_custom_call" | custom-call | flops 536870912 | bytes 8388608 | tf_op jit(solution)/shard_map/pallas_call | solution.py:166
  18.6 0.1 collective-permute-start
  18.6 1.5 %collective-permute-done = bf16[16,64,128]{2,1,0:T(8,128)(2,1)S(1)} collective-permute-done((bf16[16,64,128]{2,1,0:T(8,128)(2,1)S(1)}, bf16[16,64,128]{2,1,0:T(8,128)(2,1)S(1)}, u32[]{:S(2)}, u32[]{:S(2)}) %collective-permute-start) | collective-permute-done | bytes 262176 | tf_op jit(solution)/shard_map/ppermute | solution.py:190
  20.2 0.1 add_convert_fusion
  20.2 12.1 %all_to_all.11 = bf16[8,2,64,128]{3,2,1,0:T(8,128)(2,1)S(1)} all-to-all(bf16[8,2,64,128]{3,2,1,0:T(8,128)(2,1)S(1)} %bitcast.17), channel_id=1, replica_groups={{0,2,4,6,8,10,12,14},{1,3,5,7,9,11,13,15},{16,18,20,22,24,26,28,30},{17..., dimensions={0} | all-to-all | bytes 524288 | tf_op jit(solution)/shard_map/all_to_all | solution.py:195
  32.4 1.6 %collective-permute-start.1 = (f32[256]{0:T(256)S(1)}, f32[256]{0:T(256)S(1)}, u32[]{:S(2)}, u32[]{:S(2)}) collective-permute-start(f32[256]{0:T(256)S(1)} %bitcast.20), channel_id=1, source_target_pairs={{0,16},{16,0},{1,17},{17,1},{2,18},{18,2},{3,19},{19,3},{4,20},{20... | collective-permute-start | bytes 3080 | tf_op jit(solution)/shard_map/ppermute | solution.py:201
  34.0 0.6 %copy_bitcast_fusion = f32[64,256]{1,0:T(8,128)} fusion(f32[2,64,128]{2,1,0:T(8,128)S(1)} %convert_reduce_fusion), kind=kLoop, calls=%fused_computation.4 | loop fusion | bytes 131072 | tf_op jit(solution)/shard_map/reshape | solution.py:197
  34.6 1.4 %collective-permute-done.1 = f32[256]{0:T(256)S(1)} collective-permute-done((f32[256]{0:T(256)S(1)}, f32[256]{0:T(256)S(1)}, u32[]{:S(2)}, u32[]{:S(2)}) %collective-permute-start.1) | collective-permute-done | bytes 1056 | tf_op jit(solution)/shard_map/ppermute | solution.py:201
  36.1 0.6 %add_sqrt_fusion = f32[256]{0:T(256)} fusion(f32[256]{0:T(256)S(1)} %collective-permute-done.1, f32[2,128]{1,0:T(2,128)S(1)} %multiply_reduce_fusion), kind=kLoop, calls=%fused_computation.7 | loop fusion | flops 768 | bytes 3072 | tf_op jit(solution)/shard_map/sqrt | solution.py:204
  (4 shorter events, 0.1 us)
Async XLA Ops:
  18.6 1.6 %collective-permute-start = (bf16[16,64,128]{2,1,0:T(8,128)(2,1)S(1)}, bf16[16,64,128]{2,1,0:T(8,128)(2,1)S(1)}, u32[]{:S(2)}, u32[]{:S(2)}) collective-permute-start(bf16[16,64,128]{2,1,0:T(8,128)(2,1)S(1)} %get-tuple-element.5), channel_id=1, source_target_pairs={{0,1},{1,0},{2,3},{3,2},{4,5},{5,4},{6,7},{7,6},{8,9},{9,8},{10,11... | collective-permute-start | bytes 786440 | tf_op jit(solution)/shard_map/ppermute | solution.py:190
  32.4 3.6 %collective-permute-start.1 = (f32[256]{0:T(256)S(1)}, f32[256]{0:T(256)S(1)}, u32[]{:S(2)}, u32[]{:S(2)}) collective-permute-start(f32[256]{0:T(256)S(1)} %bitcast.20), channel_id=1, source_target_pairs={{0,16},{16,0},{1,17},{17,1},{2,18},{18,2},{3,19},{19,3},{4,20},{20... | collective-permute-start | bytes 3080 | tf_op jit(solution)/shard_map/ppermute | solution.py:201
where the time goes:
time: 37.1 us; the launch traced here: 36.6 us
  blocking collectives  26.2 us (71%)
  waiting for transfers between devices  2.94 us (8%)
  Pallas kernels  2.81 us (8%)
  other arithmetic  1.71 us (5%)
  starting transfers between devices  1.65 us (4%)
  local copies, waits for them, and re-layouts  0.68 us (2%)
  between operations  0.68 us (2%)
    all_to_all x1, blocking collectives, shards(): incoming = lax.all_to_all(outgoing, 'blk', 0, 0)  14.1 us
    all_to_all x1, blocking collectives, shards(): arrived = lax.all_to_all(chip_sum, 'blk', 0, 0, axis_index_groups=same_core)  12.1 us
    pallas_call x1, Pallas kernels, shards(): pl.pallas_call(functools.partial(accumulate, groups), in_specs=[VMEM, HBM...  2.81 us
    ppermute x1, starting transfers between devices, shards(): squares = squares + lax.ppermute(squares, 'scen', [(0, 1), (1, 0)])  1.58 us
    ppermute x1, waiting for transfers between devices, shards(): across = lax.ppermute(sent, 'blk', siblings)  1.52 us
    ppermute x1, waiting for transfers between devices, shards(): squares = squares + lax.ppermute(squares, 'scen', [(0, 1), (1, 0)])  1.42 us
    convert_element_type x1, other arithmetic, shards(): (returns.astype(jnp.float32) * vol_now[None, :] / vol_hist).astype(jnp.bf...  1 us
  transfers between devices with their start and end apart: 2, of which 2 were waited for; matrix products, arithmetic and copies ran while one was open for 2% of the time, Pallas kernels for 0%

commit v1 on v0

--- a/solution.py
+++ b/solution.py
@@ -9,7 +9,7 @@
 
 UNROLL = 32
 SIZES = (4, 2, 2, 4, 2, 2)
-LAG = 6
+LAG = 4
 AHEAD = 2
 PIECES = 4
 VMEM_LIMIT = 32 * 1024 * 1024
@@ -43,9 +43,10 @@
 
     get_order = pltpu.make_async_copy(order_hbm, order, small.at[0])
     get_pairs = pltpu.make_async_copy(pairs_hbm, pairs.at[:, pl.ds(0, slots)], small.at[1])
+    begin(0, 0)
+    get_pairs.start()
     get_order.start()
-    get_pairs.start()
-    for c in range(AHEAD):
+    for c in range(1, AHEAD):
         begin(c, 0)
     acc[...] = jnp.zeros_like(acc)
     position[books] = books

time: 37.1 us -> 37.6 us (1.013); the launches traced: 36.6 us -> 37.8 us
  starting transfers between devices: 1.65 us -> 3.12 us
    ppermute x1, starting transfers between devices: 0.07 us -> 1.53 us  [shards(): across = lax.ppermute(sent, 'blk', siblings)]
where the time goes in v1:
time: 37.6 us; the launch traced here: 37.8 us
  blocking collectives  26.2 us (70%)
  starting transfers between devices  3.12 us (8%)
  Pallas kernels  2.86 us (8%)
  waiting for transfers between devices  2.58 us (7%)
  other arithmetic  1.71 us (5%)
  local copies, waits for them, and re-layouts  0.68 us (2%)
  between operations  0.67 us (2%)
    all_to_all x1, blocking collectives, shards(): incoming = lax.all_to_all(outgoing, 'blk', 0, 0)  14.1 us
    all_to_all x1, blocking collectives, shards(): arrived = lax.all_to_all(chip_sum, 'blk', 0, 0, axis_index_groups=same_core)  12.2 us
    pallas_call x1, Pallas kernels, shards(): pl.pallas_call(functools.partial(accumulate, groups), in_specs=[VMEM, HBM...  2.86 us
    ppermute x1, starting transfers between devices, shards(): squares = squares + lax.ppermute(squares, 'scen', [(0, 1), (1, 0)])  1.58 us
    ppermute x1, starting transfers between devices, shards(): across = lax.ppermute(sent, 'blk', siblings)  1.53 us
    ppermute x1, waiting for transfers between devices, shards(): squares = squares + lax.ppermute(squares, 'scen', [(0, 1), (1, 0)])  1.41 us
    ppermute x1, waiting for transfers between devices, shards(): across = lax.ppermute(sent, 'blk', siblings)  1.16 us
    convert_element_type x1, other arithmetic, shards(): (returns.astype(jnp.float32) * vol_now[None, :] / vol_hist).astype(jnp.bf...  1 us
  transfers between devices with their start and end apart: 2, of which 2 were waited for; matrix products, arithmetic and copies ran while one was open for 2% of the time, Pallas kernels for 0%

profile of v1, /device:TPU:0, one launch (start us, length us, event | category | flops | bytes accessed | tf_op | source)
XLA Modules:
  0.0 37.8 jit_solution(7938984379881960513)
XLA Ops:
  0.6 1.0 %fusion = bf16[4,8192]{1,0:T(4,128)(2,1)S(1)} fusion(f32[4,8192]{1,0:T(4,128)} %param.7, bf16[4,8192]{1,0:T(4,128)(2,1)} %param.6, f32[8192]{0:T(1024)} %param.8), kind=kLoop, calls=%fused_computation.3 | loop fusion | flops 131072 | bytes 294912 | tf_op jit(solution)/shard_map/convert_element_type | solution.py:162
  1.6 14.1 %all_to_all.10 = bf16[16,4,512]{2,1,0:T(4,128)(2,1)S(1)} all-to-all(bf16[16,4,512]{2,1,0:T(4,128)(2,1)S(1)} %bitcast.18), channel_id=1, replica_groups=mesh['scen'=2,'blk'=16] {'blk'}, dimensions={0} | all-to-all | bytes 131072 | tf_op jit(solution)/shard_map/all_to_all | solution.py:164
  15.7 2.9 %shard_map.77 = (f32[16,64,128]{2,1,0:T(8,128)S(1)}, bf16[16,64,128]{2,1,0:T(8,128)(2,1)S(1)}) custom-call(bf16[4,64,128]{2,1,0:T(8,128)(2,1)S(1)} %bitcast.16, s32[3,256]{1,0:T(4,128)} %bitcast.19, s32[32]{0:T(128)} %order_hbm.1, bf16[256,128,128]{2,1,0:T(8,128)(2,1)} %sens_hbm.1), custom_call_target="tpu_custom_call" | custom-call | flops 536870912 | bytes 8388608 | tf_op jit(solution)/shard_map/pallas_call | solution.py:167
  18.6 1.5 %collective-permute-start = (bf16[16,64,128]{2,1,0:T(8,128)(2,1)S(1)}, bf16[16,64,128]{2,1,0:T(8,128)(2,1)S(1)}, u32[]{:S(2)}, u32[]{:S(2)}) collective-permute-start(bf16[16,64,128]{2,1,0:T(8,128)(2,1)S(1)} %get-tuple-element.5), channel_id=1, source_target_pairs={{0,1},{1,0},{2,3},{3,2},{4,5},{5,4},{6,7},{7,6},{8,9},{9,8},{10,11... | collective-permute-start | bytes 786440 | tf_op jit(solution)/shard_map/ppermute | solution.py:191
  20.1 1.2 %collective-permute-done = bf16[16,64,128]{2,1,0:T(8,128)(2,1)S(1)} collective-permute-done((bf16[16,64,128]{2,1,0:T(8,128)(2,1)S(1)}, bf16[16,64,128]{2,1,0:T(8,128)(2,1)S(1)}, u32[]{:S(2)}, u32[]{:S(2)}) %collective-permute-start) | collective-permute-done | bytes 262176 | tf_op jit(solution)/shard_map/ppermute | solution.py:191
  21.3 0.1 add_convert_fusion
  21.4 12.2 %all_to_all.11 = bf16[8,2,64,128]{3,2,1,0:T(8,128)(2,1)S(1)} all-to-all(bf16[8,2,64,128]{3,2,1,0:T(8,128)(2,1)S(1)} %bitcast.17), channel_id=1, replica_groups={{0,2,4,6,8,10,12,14},{1,3,5,7,9,11,13,15},{16,18,20,22,24,26,28,30},{17..., dimensions={0} | all-to-all | bytes 524288 | tf_op jit(solution)/shard_map/all_to_all | solution.py:196
  33.6 1.6 %collective-permute-start.1 = (f32[256]{0:T(256)S(1)}, f32[256]{0:T(256)S(1)}, u32[]{:S(2)}, u32[]{:S(2)}) collective-permute-start(f32[256]{0:T(256)S(1)} %bitcast.20), channel_id=1, source_target_pairs={{0,16},{16,0},{1,17},{17,1},{2,18},{18,2},{3,19},{19,3},{4,20},{20... | collective-permute-start | bytes 3080 | tf_op jit(solution)/shard_map/ppermute | solution.py:202
  35.2 0.6 %copy_bitcast_fusion = f32[64,256]{1,0:T(8,128)} fusion(f32[2,64,128]{2,1,0:T(8,128)S(1)} %convert_reduce_fusion), kind=kLoop, calls=%fused_computation.4 | loop fusion | bytes 131072 | tf_op jit(solution)/shard_map/reshape | solution.py:198
  35.8 1.4 %collective-permute-done.1 = f32[256]{0:T(256)S(1)} collective-permute-done((f32[256]{0:T(256)S(1)}, f32[256]{0:T(256)S(1)}, u32[]{:S(2)}, u32[]{:S(2)}) %collective-permute-start.1) | collective-permute-done | bytes 1056 | tf_op jit(solution)/shard_map/ppermute | solution.py:202
  37.2 0.6 %add_sqrt_fusion = f32[256]{0:T(256)} fusion(f32[256]{0:T(256)S(1)} %collective-permute-done.1, f32[2,128]{1,0:T(2,128)S(1)} %multiply_reduce_fusion), kind=kLoop, calls=%fused_computation.7 | loop fusion | flops 768 | bytes 3072 | tf_op jit(solution)/shard_map/sqrt | solution.py:205
  (4 shorter events, 0.1 us)
Async XLA Ops:
  18.6 2.7 %collective-permute-start = (bf16[16,64,128]{2,1,0:T(8,128)(2,1)S(1)}, bf16[16,64,128]{2,1,0:T(8,128)(2,1)S(1)}, u32[]{:S(2)}, u32[]{:S(2)}) collective-permute-start(bf16[16,64,128]{2,1,0:T(8,128)(2,1)S(1)} %get-tuple-element.5), channel_id=1, source_target_pairs={{0,1},{1,0},{2,3},{3,2},{4,5},{5,4},{6,7},{7,6},{8,9},{9,8},{10,11... | collective-permute-start | bytes 786440 | tf_op jit(solution)/shard_map/ppermute | solution.py:191
  33.6 3.6 %collective-permute-start.1 = (f32[256]{0:T(256)S(1)}, f32[256]{0:T(256)S(1)}, u32[]{:S(2)}, u32[]{:S(2)}) collective-permute-start(f32[256]{0:T(256)S(1)} %bitcast.20), channel_id=1, source_target_pairs={{0,16},{16,0},{1,17},{17,1},{2,18},{18,2},{3,19},{19,3},{4,20},{20... | collective-permute-start | bytes 3080 | tf_op jit(solution)/shard_map/ppermute | solution.py:202

commit v2 on v0

--- a/solution.py
+++ b/solution.py
@@ -9,7 +9,7 @@
 
 UNROLL = 32
 SIZES = (4, 2, 2, 4, 2, 2)
-LAG = 6
+LAG = 8
 AHEAD = 2
 PIECES = 4
 VMEM_LIMIT = 32 * 1024 * 1024

time: 37.1 us -> 37 us (level)
  no operation moved by 1% of the time
where the time goes in v2:
time: 37 us; the launch traced here: 36.8 us
  blocking collectives  26 us (70%)
  Pallas kernels  3.17 us (9%)
  waiting for transfers between devices  2.94 us (8%)
  other arithmetic  1.71 us (5%)
  starting transfers between devices  1.65 us (4%)
  local copies, waits for them, and re-layouts  0.68 us (2%)
  between operations  0.68 us (2%)
    all_to_all x1, blocking collectives, shards(): incoming = lax.all_to_all(outgoing, 'blk', 0, 0)  14.1 us
    all_to_all x1, blocking collectives, shards(): arrived = lax.all_to_all(chip_sum, 'blk', 0, 0, axis_index_groups=same_core)  11.9 us
    pallas_call x1, Pallas kernels, shards(): pl.pallas_call(functools.partial(accumulate, groups), in_specs=[VMEM, HBM...  3.17 us
    ppermute x1, starting transfers between devices, shards(): squares = squares + lax.ppermute(squares, 'scen', [(0, 1), (1, 0)])  1.58 us
    ppermute x1, waiting for transfers between devices, shards(): across = lax.ppermute(sent, 'blk', siblings)  1.52 us
    ppermute x1, waiting for transfers between devices, shards(): squares = squares + lax.ppermute(squares, 'scen', [(0, 1), (1, 0)])  1.42 us
    convert_element_type x1, other arithmetic, shards(): (returns.astype(jnp.float32) * vol_now[None, :] / vol_hist).astype(jnp.bf...  1 us
  transfers between devices with their start and end apart: 2, of which 2 were waited for; matrix products, arithmetic and copies ran while one was open for 2% of the time, Pallas kernels for 0%

profile of v2, /device:TPU:0, one launch (start us, length us, event | category | flops | bytes accessed | tf_op | source)
XLA Modules:
  0.0 36.8 jit_solution(5309573978020601384)
XLA Ops:
  0.6 1.0 %fusion = bf16[4,8192]{1,0:T(4,128)(2,1)S(1)} fusion(f32[4,8192]{1,0:T(4,128)} %param.7, bf16[4,8192]{1,0:T(4,128)(2,1)} %param.6, f32[8192]{0:T(1024)} %param.8), kind=kLoop, calls=%fused_computation.3 | loop fusion | flops 131072 | bytes 294912 | tf_op jit(solution)/shard_map/convert_element_type | solution.py:161
  1.6 14.1 %all_to_all.10 = bf16[16,4,512]{2,1,0:T(4,128)(2,1)S(1)} all-to-all(bf16[16,4,512]{2,1,0:T(4,128)(2,1)S(1)} %bitcast.18), channel_id=1, replica_groups=mesh['scen'=2,'blk'=16] {'blk'}, dimensions={0} | all-to-all | bytes 131072 | tf_op jit(solution)/shard_map/all_to_all | solution.py:163
  15.7 3.2 %shard_map.77 = (f32[16,64,128]{2,1,0:T(8,128)S(1)}, bf16[16,64,128]{2,1,0:T(8,128)(2,1)S(1)}) custom-call(bf16[4,64,128]{2,1,0:T(8,128)(2,1)S(1)} %bitcast.16, s32[3,256]{1,0:T(4,128)} %bitcast.19, s32[32]{0:T(128)} %order_hbm.1, bf16[256,128,128]{2,1,0:T(8,128)(2,1)} %sens_hbm.1), custom_call_target="tpu_custom_call" | custom-call | flops 536870912 | bytes 8388608 | tf_op jit(solution)/shard_map/pallas_call | solution.py:166
  18.9 0.1 collective-permute-start
  19.0 1.5 %collective-permute-done = bf16[16,64,128]{2,1,0:T(8,128)(2,1)S(1)} collective-permute-done((bf16[16,64,128]{2,1,0:T(8,128)(2,1)S(1)}, bf16[16,64,128]{2,1,0:T(8,128)(2,1)S(1)}, u32[]{:S(2)}, u32[]{:S(2)}) %collective-permute-start) | collective-permute-done | bytes 262176 | tf_op jit(solution)/shard_map/ppermute | solution.py:190
  20.5 0.1 add_convert_fusion
  20.6 11.9 %all_to_all.11 = bf16[8,2,64,128]{3,2,1,0:T(8,128)(2,1)S(1)} all-to-all(bf16[8,2,64,128]{3,2,1,0:T(8,128)(2,1)S(1)} %bitcast.17), channel_id=1, replica_groups={{0,2,4,6,8,10,12,14},{1,3,5,7,9,11,13,15},{16,18,20,22,24,26,28,30},{17..., dimensions={0} | all-to-all | bytes 524288 | tf_op jit(solution)/shard_map/all_to_all | solution.py:195
  32.6 1.6 %collective-permute-start.1 = (f32[256]{0:T(256)S(1)}, f32[256]{0:T(256)S(1)}, u32[]{:S(2)}, u32[]{:S(2)}) collective-permute-start(f32[256]{0:T(256)S(1)} %bitcast.20), channel_id=1, source_target_pairs={{0,16},{16,0},{1,17},{17,1},{2,18},{18,2},{3,19},{19,3},{4,20},{20... | collective-permute-start | bytes 3080 | tf_op jit(solution)/shard_map/ppermute | solution.py:201
  34.2 0.6 %copy_bitcast_fusion = f32[64,256]{1,0:T(8,128)} fusion(f32[2,64,128]{2,1,0:T(8,128)S(1)} %convert_reduce_fusion), kind=kLoop, calls=%fused_computation.4 | loop fusion | bytes 131072 | tf_op jit(solution)/shard_map/reshape | solution.py:197
  34.8 1.4 %collective-permute-done.1 = f32[256]{0:T(256)S(1)} collective-permute-done((f32[256]{0:T(256)S(1)}, f32[256]{0:T(256)S(1)}, u32[]{:S(2)}, u32[]{:S(2)}) %collective-permute-start.1) | collective-permute-done | bytes 1056 | tf_op jit(solution)/shard_map/ppermute | solution.py:201
  36.2 0.6 %add_sqrt_fusion = f32[256]{0:T(256)} fusion(f32[256]{0:T(256)S(1)} %collective-permute-done.1, f32[2,128]{1,0:T(2,128)S(1)} %multiply_reduce_fusion), kind=kLoop, calls=%fused_computation.7 | loop fusion | flops 768 | bytes 3072 | tf_op jit(solution)/shard_map/sqrt | solution.py:204
  (4 shorter events, 0.1 us)
Async XLA Ops:
  18.9 1.6 %collective-permute-start = (bf16[16,64,128]{2,1,0:T(8,128)(2,1)S(1)}, bf16[16,64,128]{2,1,0:T(8,128)(2,1)S(1)}, u32[]{:S(2)}, u32[]{:S(2)}) collective-permute-start(bf16[16,64,128]{2,1,0:T(8,128)(2,1)S(1)} %get-tuple-element.5), channel_id=1, source_target_pairs={{0,1},{1,0},{2,3},{3,2},{4,5},{5,4},{6,7},{7,6},{8,9},{9,8},{10,11... | collective-permute-start | bytes 786440 | tf_op jit(solution)/shard_map/ppermute | solution.py:190
  32.6 3.6 %collective-permute-start.1 = (f32[256]{0:T(256)S(1)}, f32[256]{0:T(256)S(1)}, u32[]{:S(2)}, u32[]{:S(2)}) collective-permute-start(f32[256]{0:T(256)S(1)} %bitcast.20), channel_id=1, source_target_pairs={{0,16},{16,0},{1,17},{17,1},{2,18},{18,2},{3,19},{19,3},{4,20},{20... | collective-permute-start | bytes 3080 | tf_op jit(solution)/shard_map/ppermute | solution.py:201

commit v3 on v0

--- a/solution.py
+++ b/solution.py
@@ -11,7 +11,7 @@
 SIZES = (4, 2, 2, 4, 2, 2)
 LAG = 6
 AHEAD = 2
-PIECES = 4
+PIECES = 2
 VMEM_LIMIT = 32 * 1024 * 1024
 VMEM = pl.BlockSpec(memory_space=pltpu.VMEM)
 HBM = pl.BlockSpec(memory_space=pltpu.HBM)

time: 37.1 us -> 37.2 us (level); the launches traced: 36.6 us -> 37.2 us
  no operation moved by 1% of the time
where the time goes in v3:
time: 37.2 us
  blocking collectives  26.3 us (71%)
  Pallas kernels  3.17 us (9%)
  waiting for transfers between devices  2.94 us (8%)
  other arithmetic  1.71 us (5%)
  starting transfers between devices  1.65 us (4%)
  local copies, waits for them, and re-layouts  0.68 us (2%)
  between operations  0.68 us (2%)
    all_to_all x1, blocking collectives, shards(): incoming = lax.all_to_all(outgoing, 'blk', 0, 0)  14.1 us
    all_to_all x1, blocking collectives, shards(): arrived = lax.all_to_all(chip_sum, 'blk', 0, 0, axis_index_groups=same_core)  12.3 us
    pallas_call x1, Pallas kernels, shards(): pl.pallas_call(functools.partial(accumulate, groups), in_specs=[VMEM, HBM...  3.17 us
    ppermute x1, starting transfers between devices, shards(): squares = squares + lax.ppermute(squares, 'scen', [(0, 1), (1, 0)])  1.58 us
    ppermute x1, waiting for transfers between devices, shards(): across = lax.ppermute(sent, 'blk', siblings)  1.52 us
    ppermute x1, waiting for transfers between devices, shards(): squares = squares + lax.ppermute(squares, 'scen', [(0, 1), (1, 0)])  1.42 us
    convert_element_type x1, other arithmetic, shards(): (returns.astype(jnp.float32) * vol_now[None, :] / vol_hist).astype(jnp.bf...  1 us
  transfers between devices with their start and end apart: 2, of which 2 were waited for; matrix products, arithmetic and copies ran while one was open for 2% of the time, Pallas kernels for 0%

profile of v3, /device:TPU:0, one launch (start us, length us, event | category | flops | bytes accessed | tf_op | source)
XLA Modules:
  0.0 37.2 jit_solution(17043388279673248807)
XLA Ops:
  0.6 1.0 %fusion = bf16[4,8192]{1,0:T(4,128)(2,1)S(1)} fusion(f32[4,8192]{1,0:T(4,128)} %param.7, bf16[4,8192]{1,0:T(4,128)(2,1)} %param.6, f32[8192]{0:T(1024)} %param.8), kind=kLoop, calls=%fused_computation.3 | loop fusion | flops 131072 | bytes 294912 | tf_op jit(solution)/shard_map/convert_element_type | solution.py:161
  1.6 14.1 %all_to_all.10 = bf16[16,4,512]{2,1,0:T(4,128)(2,1)S(1)} all-to-all(bf16[16,4,512]{2,1,0:T(4,128)(2,1)S(1)} %bitcast.18), channel_id=1, replica_groups=mesh['scen'=2,'blk'=16] {'blk'}, dimensions={0} | all-to-all | bytes 131072 | tf_op jit(solution)/shard_map/all_to_all | solution.py:163
  15.7 3.2 %shard_map.77 = (f32[16,64,128]{2,1,0:T(8,128)S(1)}, bf16[16,64,128]{2,1,0:T(8,128)(2,1)S(1)}) custom-call(bf16[4,64,128]{2,1,0:T(8,128)(2,1)S(1)} %bitcast.16, s32[3,256]{1,0:T(4,128)} %bitcast.19, s32[32]{0:T(128)} %order_hbm.1, bf16[256,128,128]{2,1,0:T(8,128)(2,1)} %sens_hbm.1), custom_call_target="tpu_custom_call" | custom-call | flops 536870912 | bytes 8388608 | tf_op jit(solution)/shard_map/pallas_call | solution.py:166
  18.9 0.1 collective-permute-start
  19.0 1.5 %collective-permute-done = bf16[16,64,128]{2,1,0:T(8,128)(2,1)S(1)} collective-permute-done((bf16[16,64,128]{2,1,0:T(8,128)(2,1)S(1)}, bf16[16,64,128]{2,1,0:T(8,128)(2,1)S(1)}, u32[]{:S(2)}, u32[]{:S(2)}) %collective-permute-start) | collective-permute-done | bytes 262176 | tf_op jit(solution)/shard_map/ppermute | solution.py:190
  20.5 0.1 add_convert_fusion
  20.6 12.3 %all_to_all.11 = bf16[8,2,64,128]{3,2,1,0:T(8,128)(2,1)S(1)} all-to-all(bf16[8,2,64,128]{3,2,1,0:T(8,128)(2,1)S(1)} %bitcast.17), channel_id=1, replica_groups={{0,2,4,6,8,10,12,14},{1,3,5,7,9,11,13,15},{16,18,20,22,24,26,28,30},{17..., dimensions={0} | all-to-all | bytes 524288 | tf_op jit(solution)/shard_map/all_to_all | solution.py:195
  33.0 1.6 %collective-permute-start.1 = (f32[256]{0:T(256)S(1)}, f32[256]{0:T(256)S(1)}, u32[]{:S(2)}, u32[]{:S(2)}) collective-permute-start(f32[256]{0:T(256)S(1)} %bitcast.20), channel_id=1, source_target_pairs={{0,16},{16,0},{1,17},{17,1},{2,18},{18,2},{3,19},{19,3},{4,20},{20... | collective-permute-start | bytes 3080 | tf_op jit(solution)/shard_map/ppermute | solution.py:201
  34.5 0.6 %copy_bitcast_fusion = f32[64,256]{1,0:T(8,128)} fusion(f32[2,64,128]{2,1,0:T(8,128)S(1)} %convert_reduce_fusion), kind=kLoop, calls=%fused_computation.4 | loop fusion | bytes 131072 | tf_op jit(solution)/shard_map/reshape | solution.py:197
  35.2 1.4 %collective-permute-done.1 = f32[256]{0:T(256)S(1)} collective-permute-done((f32[256]{0:T(256)S(1)}, f32[256]{0:T(256)S(1)}, u32[]{:S(2)}, u32[]{:S(2)}) %collective-permute-start.1) | collective-permute-done | bytes 1056 | tf_op jit(solution)/shard_map/ppermute | solution.py:201
  36.6 0.6 %add_sqrt_fusion = f32[256]{0:T(256)} fusion(f32[256]{0:T(256)S(1)} %collective-permute-done.1, f32[2,128]{1,0:T(2,128)S(1)} %multiply_reduce_fusion), kind=kLoop, calls=%fused_computation.7 | loop fusion | flops 768 | bytes 3072 | tf_op jit(solution)/shard_map/sqrt | solution.py:204
  (4 shorter events, 0.1 us)
Async XLA Ops:
  18.9 1.6 %collective-permute-start = (bf16[16,64,128]{2,1,0:T(8,128)(2,1)S(1)}, bf16[16,64,128]{2,1,0:T(8,128)(2,1)S(1)}, u32[]{:S(2)}, u32[]{:S(2)}) collective-permute-start(bf16[16,64,128]{2,1,0:T(8,128)(2,1)S(1)} %get-tuple-element.5), channel_id=1, source_target_pairs={{0,1},{1,0},{2,3},{3,2},{4,5},{5,4},{6,7},{7,6},{8,9},{9,8},{10,11... | collective-permute-start | bytes 786440 | tf_op jit(solution)/shard_map/ppermute | solution.py:190
  33.0 3.6 %collective-permute-start.1 = (f32[256]{0:T(256)S(1)}, f32[256]{0:T(256)S(1)}, u32[]{:S(2)}, u32[]{:S(2)}) collective-permute-start(f32[256]{0:T(256)S(1)} %bitcast.20), channel_id=1, source_target_pairs={{0,16},{16,0},{1,17},{17,1},{2,18},{18,2},{3,19},{19,3},{4,20},{20... | collective-permute-start | bytes 3080 | tf_op jit(solution)/shard_map/ppermute | solution.py:201
